TPU v7x, 256 devices: a whole 4x4x8 slice. The times are simulated.
256 devices in a mesh: dap: 64 (over y, z, x_lo), head: 4 (over x_hi, core).
Axes of the slice: x: 4 (x_hi: 2, x_lo: 2; x = x_hi * 2 + x_lo), y: 4, z: 8, core: 2. Of those that a mesh axis runs over, the one named last changes fastest.
Arguments:
- lineup_embedding: float32 [256, 1024, 256], P('dap'), may hold values from -6 to 6
- pairwise_state: float32 [1024, 1024, 128], P('dap', 'head'), may hold values from -6 to 6
- lineup_scaling_coefficients: float32 [256], replicated, may hold values from 0.1 to 1.9
- focus_projection_matrix: float32 [4, 256, 256], P(None, None, 'head'), may hold values from -0.375 to 0.375
- attention_gate_bias: float32 [256], P('head'), may hold values from -4 to 4
- focus_merge_matrix: float32 [256, 256], P('head'), may hold values from -0.375 to 0.375
- pairwise_bias_weight: float32 [128, 8], replicated, may hold values from -0.5 to 0.5
- relative_bias_table: float32 [66, 8], replicated, may hold values from -4 to 250
- tensor_operand_matrices: float32 [2, 256, 32], replicated, may hold values from -0.375 to 0.375
- outer_output_weight: float32 [1024, 128], replicated, may hold values from -1.5 to 1.5
- outer_output_bias: float32 [128], replicated, may hold values from -4 to 4
- lineup_member_flags: int32 [256], replicated, may hold values 0 or 1
- residue_presence_mask: int32 [1024], replicated, may hold values 0 or 1
- chain_label: int32 [1024], replicated, may hold values from 0 to 3, never falling along the last dimension, each value on 1 to 512 neighbouring positions
- residue_numbering: int32 [1024], replicated, may hold values from 0 to 1535, as said below
Outputs:
- alignment_state_next: float32 [256, 1024, 256], P('dap')
- pairwise_state_next: float32 [1024, 1024, 128], P('dap', 'head')
Inputs may be any that keep to these rules, and one draw needn't show every extreme that they name: `residue_numbering`: starts at 0 and rises by 1 or 2 from each residue to the next, by 2 at exactly 512 of the steps.
All inputs are finite; a program needn't handle non-finite values.
Results may differ from a plain program's by a relative error of at most 0.0003.
Values sent between devices are 32-bit elements; how exact they have to be, the bound alone decides.
No kernel may reach another device: no remote copies, remote signals or barrier semaphores. Data moves between devices by JAX's collectives and lax.ppermute only.
A program may use at most 128 MiB of HBM per device.

v0:
```python
from functools import partial
import math

import jax
import jax.numpy as jnp
from jax import lax
from jax.sharding import PartitionSpec as P

GROUP_FEATURES = 32
BUCKETS = 66


precise_einsum = partial(jnp.einsum, precision=lax.Precision.HIGHEST)


def layer_normalize(values):
    center = values - jnp.mean(values, axis=-1, keepdims=True)
    spread = jnp.mean(center * center, axis=-1, keepdims=True)
    return center * lax.rsqrt(spread + 1e-05)


def relative_buckets(index_rows, index_cols, chain_rows, chain_cols):
    reach = (BUCKETS - 2) // 2
    offset = jnp.clip(index_rows[:, None] - index_cols[None, :], -reach, reach) + reach
    return jnp.where(chain_rows[:, None] == chain_cols[None, :], offset, BUCKETS - 1)


def bias_block(
    pair_rows,
    index_rows,
    index_cols,
    chain_rows,
    chain_cols,
    pairwise_bias_weight,
    relative_bias_table,
):
    normalized_input = layer_normalize(pair_rows)
    linear = precise_einsum("ijc,ch->hij", normalized_input, pairwise_bias_weight)
    buckets = relative_buckets(index_rows, index_cols, chain_rows, chain_cols)
    onehot = (buckets[:, :, None] == jnp.arange(BUCKETS)[None, None, :]).astype(jnp.float32)
    return linear + precise_einsum("ijb,bh->hij", onehot, relative_bias_table)


def row_attention(
    alignment_row,
    pairwise_head_bias,
    key_presence_mask,
    lineup_scaling_coefficients,
    focus_projection_matrix,
    attention_gate_bias,
):
    normalized_input = layer_normalize(alignment_row) * lineup_scaling_coefficients
    projected_input = precise_einsum("ic,tcf->tif", normalized_input, focus_projection_matrix)
    heads_number = focus_projection_matrix.shape[2] // GROUP_FEATURES
    query_key_value_gate = projected_input.reshape(
        4, alignment_row.shape[0], heads_number, GROUP_FEATURES
    )
    logits = precise_einsum(
        "ihd,jhd->hij", query_key_value_gate[0], query_key_value_gate[1]
    ) / math.sqrt(GROUP_FEATURES)
    logits = logits + pairwise_head_bias + key_presence_mask[None, None, :]
    weights = jax.nn.softmax(logits, axis=-1)
    attention_output = precise_einsum("hij,jhd->ihd", weights, query_key_value_gate[2])
    gate_activations = jax.nn.sigmoid(
        query_key_value_gate[3] + attention_gate_bias.reshape(heads_number, GROUP_FEATURES)
    )
    return (gate_activations * attention_output).reshape(
        alignment_row.shape[0], heads_number * GROUP_FEATURES
    )


def outer_factor_pair(alignment_rows, tensor_operand_matrices, row_mask_slice):
    normalized_input = layer_normalize(alignment_rows)
    factors = precise_einsum("sic,tce->tsie", normalized_input, tensor_operand_matrices)
    return (factors[0] * row_mask_slice[..., None], factors[1] * row_mask_slice[..., None])


def per_device(
    lineup_embedding,
    pairwise_state,
    lineup_scaling_coefficients,
    focus_projection_matrix,
    attention_gate_bias,
    focus_merge_matrix,
    pairwise_bias_weight,
    relative_bias_table,
    tensor_operand_matrices,
    outer_output_weight,
    outer_output_bias,
    lineup_member_flags,
    residue_presence_mask,
    chain_label,
    residue_numbering,
):
    dap_index = lax.axis_index("dap")
    head_index = lax.axis_index("head")
    block_rows = pairwise_state.shape[0]
    quarter = pairwise_state.shape[1]
    sequence_rows = lineup_embedding.shape[0]
    row_start = dap_index * block_rows
    col_start = head_index * quarter
    index_rows = lax.dynamic_slice_in_dim(residue_numbering, row_start, block_rows)
    index_cols = lax.dynamic_slice_in_dim(residue_numbering, col_start, quarter)
    chain_rows = lax.dynamic_slice_in_dim(chain_label, row_start, block_rows)
    chain_cols = lax.dynamic_slice_in_dim(chain_label, col_start, quarter)
    local_bias = bias_block(
        pairwise_state,
        index_rows,
        index_cols,
        chain_rows,
        chain_cols,
        pairwise_bias_weight,
        relative_bias_table,
    )
    stacked = lax.all_gather(local_bias, "dap", axis=1, tiled=True)
    pairwise_head_bias = lax.all_to_all(stacked, "head", split_axis=0, concat_axis=2, tiled=True)
    residue_count_float = residue_presence_mask.astype(jnp.float32)
    row_count_float = lineup_member_flags.astype(jnp.float32)
    key_presence_mask = (residue_count_float - 1.0) * 1000000000.0
    gated_output = lax.map(
        lambda alignment_row: row_attention(
            alignment_row,
            pairwise_head_bias,
            key_presence_mask,
            lineup_scaling_coefficients,
            focus_projection_matrix,
            attention_gate_bias,
        ),
        lineup_embedding,
    )
    branch_terms = precise_einsum("amk,ku->amu", gated_output, focus_merge_matrix)
    device_rows = lax.dynamic_slice_in_dim(
        row_count_float, dap_index * sequence_rows, sequence_rows
    )
    outer_product_sum = lax.psum(branch_terms, "head")
    alignment_state_next = lineup_embedding + outer_product_sum
    first_operand, right_factor = outer_factor_pair(
        alignment_state_next,
        tensor_operand_matrices,
        device_rows[:, None] * residue_count_float[None, :],
    )
    factor_cols = lax.dynamic_slice_in_dim(right_factor, col_start, quarter, 1)
    column_factors = lax.all_to_all(first_operand, "dap", split_axis=1, concat_axis=0, tiled=True)
    factor_width = first_operand.shape[2]
    initial = jnp.zeros((block_rows, quarter, factor_width, factor_width), jnp.float32)
    gathered = lax.all_gather(factor_cols, "dap", axis=0, tiled=True)
    a_piece = lax.slice_in_dim(column_factors, 0, gathered.shape[0], axis=0)
    outer_sum = initial + precise_einsum("sic,sje->ijce", a_piece, gathered)
    projected_input = (
        precise_einsum(
            "ijf,fz->ijz",
            outer_sum.reshape(block_rows, quarter, factor_width * factor_width),
            outer_output_weight,
        )
        + outer_output_bias
    )
    res_rows = lax.dynamic_slice_in_dim(residue_count_float, row_start, block_rows)
    res_cols = lax.dynamic_slice_in_dim(residue_count_float, col_start, quarter)
    pair_count = res_rows[:, None] * res_cols[None, :] * jnp.sum(row_count_float)
    pairwise_state_next = pairwise_state + projected_input / jnp.maximum(pair_count, 1.0)[..., None]
    return (alignment_state_next, pairwise_state_next)


def solution(mesh):
    placed = (
        P("dap", None, None),
        P("dap", "head", None),
        P(),
        P(None, None, "head"),
        P("head"),
        P("head", None),
        P(),
        P(),
        P(),
        P(),
        P(),
        P(),
        P(),
        P(),
        P(),
    )
    return jax.shard_map(
        per_device,
        mesh=mesh,
        in_specs=placed,
        out_specs=(P("dap", None, None), P("dap", "head", None)),
        check_vma=False,
    )
```

profile of v0, /device:TPU:4, one launch (start us, length us, event | category | flops | bytes accessed | tf_op | source)
XLA Modules:
  0.0 1072.6 jit_solution(15430934260201918952)
XLA Ops:
  12.7 2.5 multiply_reduce_fusion.2
  15.8 3.5 fusion.36
  19.3 317.6 %all-gather.3.cloned.1.call-done = f32[8,1024,256]{2,0,1:T(8,128)} async-done(((f32[8,16,256]{2,0,1:T(8,128)}), f32[8,1024,256]{2,0,1:T(8,128)}) %all-gather.3.cloned.1.call-update) | async-done | bytes 8388624 | tf_op jit(solution)/shard_map/all_gather | solution.py:115
  336.9 9.3 copy.32
  346.2 6.2 all-to-all-start
  352.6 91.3 %all-to-all-done = f32[8,1024,256]{2,1,0:T(8,128)} async-done(((f32[8,1024,256]{2,1,0:T(8,128)}), f32[8,1024,256]{2,1,0:T(8,128)}, u32[]{:S(2)}, u32[]{:S(2)}) %all-to-all-start) | async-done | bytes 8388640 | tf_op jit(solution)/shard_map/all_to_all | solution.py:116
  444.0 8.8 copy.33
  452.8 112.4 %while.10 = (s32[]{:T(128)}, f32[4,1024,64]{1,2,0:T(8,128)}, f32[4,1024,256]{2,1,0:T(8,128)}, f32[256]{0:T(256)S(1)}, f32[4,256,64]{1,2,0:T(8,128)S(1)}, /*index...) while((s32[]{:T(128)}, f32[4,1024,64]{1,2,0:T(8,128)}, ...), condition=%wide.region_7.8_spmd, body=%wide.region_2.7_spmd.sunk | while | flops 2434855936 | bytes 75582336 | solution.py:120
  455.9 2.5 fusion.76
  458.5 10.1 fusion.78
  471.9 8.2 fusion.80
  483.9 2.5 fusion.76
  486.5 10.1 fusion.78
  500.0 8.2 fusion.80
  512.0 2.5 fusion.76
  514.6 10.1 fusion.78
  528.0 8.2 fusion.80
  542.6 10.1 fusion.78
  556.1 8.2 fusion.80
  565.3 6.7 fusion.46
  572.2 91.3 %all-reduce.2.cloned.1.call-done = f32[4,1024,256]{2,1,0:T(8,128)} async-done(((f32[4,1024,256]{2,1,0:T(8,128)}), f32[4,1024,256]{2,1,0:T(8,128)}) %all-reduce.2.cloned.1.call-update) | async-done | bytes 4194320 | tf_op jit(solution)/shard_map/psum | solution.py:135
  663.6 4.2 fusion.50
  669.1 5.2 fusion.29
  678.9 3.5 reshape.185
  682.4 12.8 %all-to-all-start.1 = ((f32[64,1,2048]{2,1,0:T(1,128)}), f32[64,1,2048]{2,1,0:T(1,128)S(1)}, u32[]{:S(2)}, u32[]{:S(2)}) async-start(f32[64,1,2048]{2,1,0:T(1,128)} %reshape.185), calls=%async_computation.1 | async-start | bytes 1048576 | tf_op jit(solution)/shard_map/all_to_all | solution.py:143
  696.6 22.2 %all-to-all-done.1 = f32[64,1,2048]{2,1,0:T(1,128)S(1)} async-done(((f32[64,1,2048]{2,1,0:T(1,128)}), f32[64,1,2048]{2,1,0:T(1,128)S(1)}, u32[]{:S(2)}, u32[]{:S(2)}) %all-to-all-start.1) | async-done | bytes 524320 | tf_op jit(solution)/shard_map/all_to_all | solution.py:143
  720.1 2.9 reduce.1
  728.8 2.5 copy.39
  731.3 264.3 %all-gather.5.cloned.1.call-done = f32[256,256,32]{1,2,0:T(8,128)} async-done(((f32[4,256,32]{1,2,0:T(8,128)}), f32[256,256,32]{1,2,0:T(8,128)}) %all-gather.5.cloned.1.call-update) | async-done | bytes 8388624 | tf_op jit(solution)/shard_map/all_gather | solution.py:146
  995.6 23.3 %convolution_bitcast_fusion = f32[16,256,32,32]{1,2,0,3:T(8,128)S(1)} fusion(f32[256,256,32,1]{1,2,0,3:T(8,128)} %bitcast.112, f32[256,16,32]{0,2,1:T(8,128)S(1)} %copy.39), kind=kOutput, calls=%fused_computation.23 | convolution fusion | flops 12884901888 | bytes 25690112 | tf_op jit(solution)/shard_map/sic,sje->ijce/dot_general | solution.py:148
  1018.9 18.3 %copy.40 = f32[16,256,32,32]{1,3,2,0:T(8,128)S(1)} copy(f32[16,256,32,32]{1,2,0,3:T(8,128)S(1)} %convolution_bitcast_fusion) | data formatting | bytes 33554432 | tf_op jit(solution)/shard_map/sic,sje->ijce/transpose | solution.py:148
  1037.2 28.6 %divide_add_fusion = f32[16,256,128]{2,1,0:T(8,128)} fusion(f32[16,256,128]{2,1,0:T(8,128)S(1)} %copy-done.2, f32[16,256,1024]{1,2,0:T(8,128)S(1)} %bitcast.108, f32[16,256]{1,0:T(8,128)S(1)} %multiply_maximum_fusion, f32[128]{0:T(128)S(1)} %copy-done.12, f32[1024,128]{1,0:T(8,128)S(1)} %copy-done), kind=kOutput, calls=%fused_computation.30 | convolution fusion | flops 6444023808 | bytes 21512704 | tf_op jit(solution)/shard_map/ijf,fz->ijz/dot_general | solution.py:150
  (108 shorter events, 52.0 us)
Async XLA Ops:
  7.2 1030.0 %copy-start = (f32[1024,128]{1,0:T(8,128)S(1)}, f32[1024,128]{1,0:T(8,128)}, u32[]{:S(2)}) copy-start(f32[1024,128]{1,0:T(8,128)} %param.26) | copy-start | bytes 1572868
  7.2 8.6 copy-start.2
  7.2 8.1 copy-start.14
  7.2 8.6 copy-start.11
  7.2 329.7 %all-gather.3.cloned.1.call-start = ((), (), s32[]{:S(2)}) async-start(), calls=%async_computation.2 | async-start | bytes 8519680 | tf_op jit(solution)/shard_map/all_gather | solution.py:115
  346.2 6.4 copy-start.10
  346.2 97.8 %all-to-all-start = ((f32[8,1024,256]{2,1,0:T(8,128)}), f32[8,1024,256]{2,1,0:T(8,128)}, u32[]{:S(2)}, u32[]{:S(2)}) async-start(f32[8,1024,256]{2,1,0:T(8,128)} %copy.32), calls=%async_computation | async-start | bytes 16777216 | tf_op jit(solution)/shard_map/all_to_all | solution.py:116
  352.4 311.1 %all-reduce.2.cloned.1.call-start = ((), (), s32[]{:S(2)}) async-start(), calls=%async_computation.3 | async-start | bytes 8388608 | tf_op jit(solution)/shard_map/psum | solution.py:135
  444.0 8.8 copy-start.4
  444.0 8.8 copy-start.9
  444.0 8.8 copy-start.15
  452.8 112.5 %copy-start.7 = (f32[64,256]{1,0:T(8,128)S(1)}, f32[64,256]{1,0:T(8,128)}, u32[]{:S(2)}) copy-start(f32[64,256]{1,0:T(8,128)} %param.22) | copy-start | bytes 196612
  468.6 3.3 copy-start.1
  496.6 3.3 copy-start.1
  524.7 3.3 copy-start.1
  552.7 3.3 copy-start.1
  565.2 6.8 copy-start.13
  572.0 423.6 %all-gather.5.cloned.1.call-start = ((), (), s32[]{:S(2)}) async-start(), calls=%async_computation.4 | async-start | bytes 8519680 | tf_op jit(solution)/shard_map/all_gather | solution.py:146
  667.7 6.7 copy-start.3
  667.7 1.4 copy-start.8
  674.4 1.0 copy-start.5
  682.4 36.5 %all-to-all-start.1 = ((f32[64,1,2048]{2,1,0:T(1,128)}), f32[64,1,2048]{2,1,0:T(1,128)S(1)}, u32[]{:S(2)}, u32[]{:S(2)}) async-start(f32[64,1,2048]{2,1,0:T(1,128)} %reshape.185), calls=%async_computation.1 | async-start | bytes 1048576 | tf_op jit(solution)/shard_map/all_to_all | solution.py:143
  718.8 0.8 copy-start.6
  1018.9 18.3 %copy-start.12 = (f32[128]{0:T(128)S(1)}, f32[128]{0:T(128)}, u32[]{:S(2)}) copy-start(f32[128]{0:T(128)} %param.27) | copy-start | bytes 1540
Sparse Core Ops, SparseCore 0:
  19.4 317.4 all-gather.2
  572.1 91.4 all-reduce.1
  676.2 319.3 all-gather.4
where the time goes:
time: 1080 us; the launch traced here: 1070 us
  waiting for transfers between devices  787 us (73%)
  matrix products  151 us (14%)
  local copies, waits for them, and re-layouts  67.5 us (6%)
  other arithmetic  33.1 us (3%)
  starting transfers between devices  19.2 us (2%)
  between operations  14.3 us (1%)
    all_gather x1, waiting for transfers between devices, per_device(): stacked = lax.all_gather(local_bias, 'dap', axis=1, tiled=True)  318 us
    all_gather x1, waiting for transfers between devices, per_device(): gathered = lax.all_gather(factor_cols, 'dap', axis=0, tiled=True)  264 us
    all_to_all x1, waiting for transfers between devices, per_device(): lax.all_to_all(stacked, 'head', split_axis=0, concat_axis=2, tiled=True)  91.3 us
    psum x1, waiting for transfers between devices, per_device(): outer_product_sum = lax.psum(branch_terms, 'head')  91.3 us
    dot_general x4, matrix products, row_attention(): precise_einsum('ihd,jhd->hij', query_key_value_gate[0], query_key_value_g...  40.5 us
    dot_general x4, matrix products, row_attention(): precise_einsum('hij,jhd->ihd', weights, query_key_value_gate[2])  32.8 us
    dot_general x1, matrix products, per_device(): precise_einsum('ijf,fz->ijz', outer_sum.reshape(block_rows, quarter, fact...  28.6 us
    dot_general x1, matrix products, per_device(): outer_sum = initial + precise_einsum('sic,sje->ijce', a_piece, gathered)  23.3 us
  transfers between devices with their start and end apart: 5, of which 5 were waited for; matrix products, arithmetic and copies ran while one was open for 2% of the time, Pallas kernels for 0%

commit v1 on v0

v1 whole, which is shorter than its diff:
```python
import math
from functools import partial

import jax
import jax.numpy as jnp
from jax import lax
from jax.experimental import pallas as pl
from jax.experimental.pallas import tpu as pltpu
from jax.sharding import Mesh, PartitionSpec as P

F32, BF16 = jnp.float32, jnp.bfloat16
HEADS, DEPTH, RANK, BUCKETS = 8, 32, 32, 66
TABLE_ROWS = 72
LANES = 128
LOG2E = math.log2(math.e)
HEAD_AXES = ("xh", "c")
DAP_AXES = ("y", "z", "xl")


def dot(a, b, contract=((1,), (0,))):
    return lax.dot_general(a, b, (contract, ((), ())), preferred_element_type=F32)


def split(a):
    high = a.astype(BF16)
    return high, (a - high.astype(F32)).astype(BF16)


def dot3(a, b, contract=((1,), (0,))):
    return dot(a[0], b[0], contract) + (dot(a[0], b[1], contract) + dot(a[1], b[0], contract))


def normalize(values):
    center = values - jnp.mean(values, axis=-1, keepdims=True)
    spread = jnp.mean(center * center, axis=-1, keepdims=True)
    return center * lax.rsqrt(spread + 1e-05)


def params(n_axes, mib):
    return pltpu.CompilerParams(
        dimension_semantics=("arbitrary",) * n_axes, vmem_limit_bytes=mib * 2**20
    )


def bias_kernel(place, index_s, chain_s, pair, weight_t, table_t, index_c, chain_c, mask_c, out):
    step = pl.program_id(0)
    rows = pair.shape[0]
    columns = pair.shape[1]
    w = weight_t[...]
    table = table_t[...]
    cols_index = index_c[0]
    cols_chain = chain_c[0]
    mask = mask_c[0]
    reach = (BUCKETS - 2) // 2
    for r in range(rows):
        i = place[0] * (rows * pl.num_programs(0)) + step * rows + r
        normed = normalize(pair[r])
        linear = lax.dot_general(
            w, normed, (((1,), (1,)), ((), ())), precision=lax.Precision.HIGHEST,
            preferred_element_type=F32,
        )
        offset = jnp.clip(index_s[i] - cols_index, -reach, reach) + reach
        bucket = jnp.where(chain_s[i] == cols_chain, offset, BUCKETS - 1)
        classes = lax.broadcasted_iota(jnp.int32, (TABLE_ROWS, columns), 0)
        onehot = (classes == bucket).astype(F32)
        relative = lax.dot_general(
            table, onehot, (((1,), (0,)), ((), ())), precision=lax.Precision.HIGHEST,
            preferred_element_type=F32,
        )
        out[:, r, :] = (linear + relative + mask) * LOG2E


def pair_bias(place, numbering, chain, mask_add, pair, weight, table):
    rows, columns, channels = pair.shape
    part = 8
    return pl.pallas_call(
        bias_kernel,
        out_shape=jax.ShapeDtypeStruct((HEADS, rows, columns), F32),
        grid_spec=pltpu.PrefetchScalarGridSpec(
            num_scalar_prefetch=3,
            grid=(rows // part,),
            in_specs=[
                pl.BlockSpec((part, columns, channels), lambda r, *_: (r, 0, 0)),
                pl.BlockSpec((HEADS, channels), lambda r, *_: (0, 0)),
                pl.BlockSpec((HEADS, TABLE_ROWS), lambda r, *_: (0, 0)),
                pl.BlockSpec((1, 1, columns), lambda r, place, *_: (place[1], 0, 0)),
                pl.BlockSpec((1, 1, columns), lambda r, place, *_: (place[1], 0, 0)),
                pl.BlockSpec((1, 1, columns), lambda r, place, *_: (place[1], 0, 0)),
            ],
            out_specs=pl.BlockSpec((HEADS, part, columns), lambda r, *_: (0, r, 0)),
        ),
        compiler_params=params(1, 32),
        name="pair_bias",
    )(
        place, numbering, chain, pair, weight.T,
        jnp.pad(table, ((0, TABLE_ROWS - BUCKETS), (0, 0))).T,
        numbering.reshape(-1, 1, columns), chain.reshape(-1, 1, columns),
        mask_add.reshape(-1, 1, columns),
    )


def project_kernel(place, row, own, gain, wk, wv, wq, wg, gate_bias, kp, vp, qp, gp,
                   wk2, wv2, wq2, wg2):
    @pl.when(pl.program_id(0) == 0)
    def _():
        for source, target in ((wk, wk2), (wv, wv2), (wq, wq2), (wg, wg2)):
            target[0], target[1] = split(source[...])

    positions = row.shape[1]
    own_positions = own.shape[1]
    n = split(normalize(row[0]) * gain[...])
    keys = split(dot3((wk2[0], wk2[1]), n, ((1,), (1,))))
    for h in range(HEADS):
        for part in range(4):
            kp[0, h, pl.ds(part * DEPTH, DEPTH), :] = keys[part % 2][h * DEPTH:(h + 1) * DEPTH]
    pair_lanes = 2 * LANES
    lane = lax.broadcasted_iota(jnp.int32, (positions, LANES), 1)
    for h in range(0, HEADS, 2):
        cut = pl.ds(h * LANES, pair_lanes)
        both = dot3(n, (wv2[0, :, cut], wv2[1, :, cut]))
        for k in range(2):
            value = both[:, k * LANES:(k + 1) * LANES]
            high = value.astype(BF16).astype(F32)
            packed = jnp.where(lane < DEPTH, high, jnp.where(lane < 2 * DEPTH, value - high, 1.0))
            vp[0, h + k] = packed.astype(BF16)
    m = split(normalize(own[0]) * gain[...])
    lane = lax.broadcasted_iota(jnp.int32, (own_positions, LANES), 1)
    for h in range(0, HEADS, 2):
        cut = pl.ds(h * LANES, pair_lanes)
        both = dot3(m, (wq2[0, :, cut], wq2[1, :, cut])) * (LOG2E / math.sqrt(DEPTH))
        gates = dot3(m, (wg2[0, :, cut], wg2[1, :, cut])) + gate_bias[:, cut]
        gates = jax.nn.sigmoid(gates)
        for k in range(2):
            value = both[:, k * LANES:(k + 1) * LANES]
            high = value.astype(BF16).astype(F32)
            qp[0, h + k] = jnp.where(lane < 2 * DEPTH, high, value - high).astype(BF16)
            gp[0, h + k] = gates[:, k * LANES:(k + 1) * LANES]


def project(place, rows, gain, wk, wv, wq, wg, gate_bias, quarter):
    count, positions, channels = rows.shape
    wide = HEADS * LANES

    def whole(shape):
        return pl.BlockSpec(shape, lambda s, place: (0,) * len(shape))

    def out(rows_, columns, dtype):
        return (
            jax.ShapeDtypeStruct((count, HEADS, rows_, columns), dtype),
            pl.BlockSpec((1, HEADS, rows_, columns), lambda s, place: (s, 0, 0, 0)),
        )

    outs = [out(LANES, positions, BF16), out(positions, LANES, BF16),
            out(quarter, LANES, BF16), out(quarter, LANES, F32)]
    return pl.pallas_call(
        project_kernel,
        out_shape=[o[0] for o in outs],
        grid_spec=pltpu.PrefetchScalarGridSpec(
            num_scalar_prefetch=1,
            grid=(count,),
            in_specs=[
                pl.BlockSpec((1, positions, channels), lambda s, place: (s, 0, 0)),
                pl.BlockSpec((1, quarter, channels), lambda s, place: (s, place[1], 0)),
                whole((1, channels)), whole((HEADS * DEPTH, channels)),
                whole((channels, wide)), whole((channels, wide)), whole((channels, wide)),
                whole((1, wide)),
            ],
            out_specs=[o[1] for o in outs],
            scratch_shapes=[pltpu.VMEM((2, HEADS * DEPTH, channels), BF16)]
            + [pltpu.VMEM((2, channels, wide), BF16)] * 3,
        ),
        compiler_params=params(1, 52),
        name="project",
    )(place, rows, rows, gain[None], wk, wv, wq, wg, gate_bias)


def attend_kernel(place, flags_s, bias, kp, vp, qp, gp, merge, own, operand_t, mask_c,
                  state_out, first_out, second_out, total):
    h = pl.program_id(0)
    count = own.shape[0]
    positions = kp.shape[3]
    quarter = own.shape[1]
    cuts = bias.shape[1]
    width = bias.shape[5]
    m2 = split(merge[0])

    @pl.when(h == 0)
    def _():
        total[...] = jnp.zeros_like(total)

    head_bias = jnp.concatenate(
        [bias[:, y, :, 0].reshape(quarter, width) for y in range(cuts)], axis=1
    )
    for s in range(count):
        logits = dot(qp[s, 0], kp[s, 0]) + head_bias
        peak = jnp.max(logits, axis=1, keepdims=True)
        weights = jnp.exp2(logits - peak)
        high, low = split(weights)
        mixed = dot(high, vp[s, 0]) + dot(low, vp[s, 0])
        total_weight = pltpu.roll(mixed, LANES // 2, 1)
        lane = lax.broadcasted_iota(jnp.int32, mixed.shape, 1)
        total_weight = jnp.where(lane < 2 * DEPTH, total_weight, 1.0)
        gated = jnp.where(lane < 2 * DEPTH, mixed * gp[s, 0] / total_weight, 0.0)
        total[s] += dot3(split(gated), m2)

    @pl.when(h == pl.num_programs(0) - 1)
    def _():
        ops = split(operand_t[...])
        for s in range(count):
            state = own[s] + total[s]
            state_out[s] = state
            n = split(normalize(state))
            flag = flags_s[place[0] * count + s].astype(F32)
            factors = dot3(ops, n, ((1,), (1,))) * (mask_c[0] * flag)
            first_out[s] = factors[:RANK]
            for e in range(RANK):
                second_out[pl.ds(s, 1), pl.ds(e * quarter, quarter)] = factors[RANK + e:RANK + e + 1]


def attend(place, flags, bias, kp, vp, qp, gp, merge, rows, operand_t, mask, quarter):
    count, positions, channels = rows.shape
    z, y, xl, heads, i, width = bias.shape

    def head_block(rows_, columns):
        return pl.BlockSpec((count, 1, rows_, columns), lambda h, *_: (0, h, 0, 0))

    return pl.pallas_call(
        attend_kernel,
        out_shape=[
            jax.ShapeDtypeStruct((count, quarter, channels), F32),
            jax.ShapeDtypeStruct((count, RANK, quarter), F32),
            jax.ShapeDtypeStruct((count, RANK * quarter), F32),
        ],
        grid_spec=pltpu.PrefetchScalarGridSpec(
            num_scalar_prefetch=2,
            grid=(HEADS,),
            in_specs=[
                pl.BlockSpec((z, y, xl, 1, i, width), lambda h, *_: (0, 0, 0, h, 0, 0)),
                head_block(LANES, positions), head_block(positions, LANES),
                head_block(quarter, LANES), head_block(quarter, LANES),
                pl.BlockSpec((1, LANES, channels), lambda h, *_: (h, 0, 0)),
                pl.BlockSpec((count, quarter, channels), lambda h, place, *_: (0, place[1], 0)),
                pl.BlockSpec((2 * RANK, channels), lambda h, *_: (0, 0)),
                pl.BlockSpec((1, 1, quarter), lambda h, place, *_: (place[1], 0, 0)),
            ],
            out_specs=[
                pl.BlockSpec((count, quarter, channels), lambda h, *_: (0, 0, 0)),
                pl.BlockSpec((count, RANK, quarter), lambda h, *_: (0, 0, 0)),
                pl.BlockSpec((count, RANK * quarter), lambda h, *_: (0, 0)),
            ],
            scratch_shapes=[pltpu.VMEM((count, quarter, channels), F32)],
        ),
        compiler_params=params(1, 52),
        name="attend",
    )(place, flags, bias, kp, vp, qp, gp, merge, rows, operand_t, mask.reshape(-1, 1, quarter))


def outer_kernel(group, place, mask_s, first, second, weight_t, out_bias, count_c, pair, out,
                 a2, w2, r2):
    step = pl.program_id(0)
    steps = RANK // group
    i_rows = r2.shape[1]
    columns = pair.shape[1]

    @pl.when(step == 0)
    def _():
        high, low = split(first[...].T)
        a2[0], a2[1] = high, low
        high, low = split(weight_t[...])
        w2[:LANES], w2[LANES:] = high, low

    @pl.when(step < steps)
    def _():
        for g in range(group):
            b = split(second[:, g * columns:(g + 1) * columns])
            r = split(dot3((a2[0], a2[1]), b))
            at = pl.multiple_of((step * group + g) * RANK, RANK)
            for part in range(2):
                for i in range(i_rows):
                    r2[part, i, pl.ds(at, RANK), :] = r[part][i * RANK:(i + 1) * RANK]

    @pl.when(step >= steps)
    def _():
        i = step - steps
        both = dot(w2[...], r2[0, i])
        value = both[:LANES] + (both[LANES:] + dot(w2[:LANES], r2[1, i])) + out_bias[...]
        count = jnp.maximum(mask_s[place[0] * i_rows + i].astype(F32) * count_c[0], 1.0)
        out[0] = pair[0] + (value / count).T


def outer_mean(place, mask, first, second, weight_t, out_bias, count, pair):
    rows, columns, channels = pair.shape
    members = first.shape[0]
    group = 4
    steps = RANK // group

    def own(t, *_):
        return (jnp.maximum(t - steps, 0), 0, 0)

    return pl.pallas_call(
        partial(outer_kernel, group),
        out_shape=jax.ShapeDtypeStruct(pair.shape, F32),
        grid_spec=pltpu.PrefetchScalarGridSpec(
            num_scalar_prefetch=2,
            grid=(steps + rows,),
            in_specs=[
                pl.BlockSpec((members, rows * RANK), lambda t, *_: (0, 0)),
                pl.BlockSpec((members, group * columns),
                             lambda t, *_: (0, jnp.minimum(t, steps - 1))),
                pl.BlockSpec((channels, RANK * RANK), lambda t, *_: (0, 0)),
                pl.BlockSpec((channels, 1), lambda t, *_: (0, 0)),
                pl.BlockSpec((1, 1, columns), lambda t, place, *_: (place[1], 0, 0)),
                pl.BlockSpec((1, columns, channels), own),
            ],
            out_specs=pl.BlockSpec((1, columns, channels), own),
            scratch_shapes=[
                pltpu.VMEM((2, rows * RANK, members), BF16),
                pltpu.VMEM((2 * channels, RANK * RANK), BF16),
                pltpu.VMEM((2, rows, RANK * RANK, columns), BF16),
            ],
        ),
        compiler_params=params(1, 52),
        name="outer_mean",
    )(place, mask, first, second, weight_t, out_bias[:, None],
      count.reshape(-1, 1, columns), pair)


def in_order(mine, other):
    low = lax.axis_index("xl") == 0
    return jnp.stack([jnp.where(low, mine, other), jnp.where(low, other, mine)])


def per_device(
    sizes,
    lineup_embedding,
    pairwise_state,
    lineup_scaling_coefficients,
    focus_projection_matrix,
    attention_gate_bias,
    focus_merge_matrix,
    pairwise_bias_weight,
    relative_bias_table,
    tensor_operand_matrices,
    outer_output_weight,
    outer_output_bias,
    lineup_member_flags,
    residue_presence_mask,
    chain_label,
    residue_numbering,
):
    ny, nz, nxl, nxh, nc = (sizes[a] for a in ("y", "z", "xl", "xh", "c"))
    nq = nxh * nc
    dap = (lax.axis_index("y") * nz + lax.axis_index("z")) * nxl + lax.axis_index("xl")
    head = lax.axis_index("xh") * nc + lax.axis_index("c")
    place = jnp.stack([dap, head]).astype(jnp.int32)
    count, positions, channels = lineup_embedding.shape
    block_rows, quarter, pair_channels = pairwise_state.shape
    presence = residue_presence_mask.astype(F32)
    key_mask = (presence - 1.0) * 1000000000.0

    narrow = focus_projection_matrix.shape[2]
    packed = jnp.concatenate(
        [
            focus_projection_matrix.reshape(-1, narrow),
            focus_merge_matrix.reshape(-1, narrow),
            jnp.broadcast_to(attention_gate_bias[None], (8, narrow)),
        ]
    )
    packed = lax.all_gather(packed, HEAD_AXES)
    weights = packed[:, :4 * channels].reshape(nq, 4, channels, narrow)
    weights = jnp.transpose(weights, (1, 2, 0, 3)).reshape(4, channels, HEADS, DEPTH)
    merge = packed[:, 4 * channels:5 * channels].reshape(HEADS, DEPTH, channels)
    gate_bias = packed[:, 5 * channels].reshape(HEADS, DEPTH)

    def lanes(a, copies):
        a = jnp.concatenate([a] * copies, axis=-1)
        a = jnp.pad(a, ((0, 0),) * (a.ndim - 1) + ((0, LANES - a.shape[-1]),))
        return a.reshape(a.shape[:-2] + (HEADS * LANES,))

    wk = weights[1].reshape(channels, HEADS * DEPTH).T
    wq, wv, wg = lanes(weights[0], 4), lanes(weights[2], 2), lanes(weights[3], 2)
    merge = jnp.pad(jnp.concatenate([merge, merge], axis=1), ((0, 0), (0, LANES - 2 * DEPTH), (0, 0)))

    local = pair_bias(place, residue_numbering, chain_label, key_mask, pairwise_state,
                      pairwise_bias_weight, relative_bias_table)

    def swap(flip):
        shape = (ny, nxl, nq)
        perm = []
        for y in range(ny):
            for x in range(nxl):
                for q in range(nq):
                    to = (q * nxl + (x ^ flip)) * nq + y
                    perm.append(((y * nxl + x) * nq + q, to))
        return perm

    cross = ("y", "xl") + HEAD_AXES
    bias = in_order(lax.ppermute(local, cross, swap(0)), lax.ppermute(local, cross, swap(1)))
    bias = lax.all_gather(bias, ("y", "z"))
    bias = jnp.swapaxes(bias.reshape((ny, nz) + bias.shape[1:]), 0, 1)

    kp, vp, qp, gp = project(place, lineup_embedding, lineup_scaling_coefficients, wk, wv, wq, wg,
                             lanes(gate_bias, 2)[None], quarter)
    operand_t = jnp.swapaxes(tensor_operand_matrices, 1, 2).reshape(2 * RANK, channels)
    state, first, second = attend(place, lineup_member_flags, bias, kp, vp, qp, gp, merge,
                                  lineup_embedding, operand_t, presence, quarter)

    flip = [(0, 1), (1, 0)]
    second = in_order(second, lax.ppermute(second, "xl", flip)).reshape(nxl * count, -1)
    second = lax.all_gather(second, ("y", "z")).reshape(ny * nz * nxl * count, -1)

    parts = nz * nxl
    first = jnp.transpose(first.reshape(count, RANK, parts, block_rows), (2, 0, 3, 1))
    first = lax.all_to_all(first.reshape(parts, count, block_rows * RANK), ("z", "xl"), 0, 0, tiled=True)
    first = lax.all_gather(first.reshape(parts * count, -1), "y")
    back = [(y * nq + q, q * nq + y) for y in range(ny) for q in range(nq)]
    first = lax.ppermute(first, ("y",) + HEAD_AXES, back)
    first = first.reshape(ny * parts * count, block_rows * RANK)

    state = lax.all_gather(state, HEAD_AXES, axis=1, tiled=True)

    weight_t = jnp.transpose(
        outer_output_weight.reshape(RANK, RANK, pair_channels), (2, 1, 0)
    ).reshape(pair_channels, RANK * RANK)
    count_columns = presence * jnp.sum(lineup_member_flags.astype(F32))
    pairs = outer_mean(place, residue_presence_mask, first, second, weight_t, outer_output_bias,
                       count_columns, pairwise_state)
    return state, pairs


def solution(mesh):
    sizes = dict(y=4, z=8, xl=2, xh=2, c=2)
    fine = Mesh(mesh.devices.reshape(tuple(sizes.values())), tuple(sizes))
    placed = (
        P(DAP_AXES, None, None),
        P(DAP_AXES, HEAD_AXES, None),
        P(),
        P(None, None, HEAD_AXES),
        P(HEAD_AXES),
        P(HEAD_AXES, None),
    ) + (P(),) * 9
    return jax.shard_map(
        partial(per_device, sizes),
        mesh=fine,
        in_specs=placed,
        out_specs=(P(DAP_AXES, None, None), P(DAP_AXES, HEAD_AXES, None)),
        check_vma=False,
    )
```

time: 1080 us -> 367 us (0.34)
  waiting for transfers between devices: 787 us -> 197 us
  matrix products: 151 us -> 0 us
  Pallas kernels: 0 us -> 82.3 us
  local copies, waits for them, and re-layouts: 67.5 us -> 26.6 us
  blocking collectives: 0 us -> 27.4 us
  other arithmetic: 33.1 us -> 5.77 us
    all_gather x2 -> x4, waiting for transfers between devices: 582 us -> 164 us  [the longest x1 92.7 us: per_device(): lax.all_gather(second, ('y', 'z')).reshape(ny * nz * nxl * count, -1)]
    dot_general x14 -> x0, matrix products: 141 us -> none  [the longest x4 40.5 us: row_attention(): precise_einsum('ihd,jhd->hij', query_key_value_gate[0], query_key_value_g...]
    all_to_all x2 -> x0, waiting for transfers between devices: 114 us -> none  [the longest x1 91.3 us: per_device(): lax.all_to_all(stacked, 'head', split_axis=0, concat_axis=2, tiled=True)]
    psum x1 -> x0, waiting for transfers between devices: 91.3 us -> none  [per_device(): outer_product_sum = lax.psum(branch_terms, 'head')]
    pallas_call x0 -> x4, Pallas kernels: none -> 82.3 us  [the longest x1 36 us: attend(): pl.pallas_call(attend_kernel, out_shape=[jax.ShapeDtypeStruct((count, qua...]
    ppermute x0 -> x4, waiting for transfers between devices: none -> 33.3 us  [the longest x1 14.6 us: per_device(): first = lax.ppermute(first, ('y',) + HEAD_AXES, back)]
    reduce_sum x17 -> x1, other arithmetic: 27.5 us -> 1.28 us  [per_device(): count_columns = presence * jnp.sum(lineup_member_flags.astype(F32))]
    all_to_all x2 -> x0, starting transfers between devices: 19 us -> none  [the longest x1 12.8 us: per_device(): lax.all_to_all(first_operand, 'dap', split_axis=1, concat_axis=0, tiled=T...]
  transfers between devices with their start and end apart: 5 -> 8, of which waited for: 5 -> 6; matrix products, arithmetic and copies ran while one was open for 2% -> 4% of each run, Pallas kernels for 0% -> 6%
where the time goes in v1:
time: 367 us; the launch traced here: 366 us
  waiting for transfers between devices  197 us (54%)
  Pallas kernels  82.3 us (22%)
  blocking collectives  27.4 us (7%)
  local copies, waits for them, and re-layouts  26.6 us (7%)
  between operations  14.1 us (4%)
  starting transfers between devices  12.5 us (3%)
  other arithmetic  5.77 us (2%)
    all_gather x1, waiting for transfers between devices, per_device(): lax.all_gather(second, ('y', 'z')).reshape(ny * nz * nxl * count, -1)  92.7 us
    all_gather x1, waiting for transfers between devices, per_device(): bias = lax.all_gather(bias, ('y', 'z'))  70.9 us
    pallas_call x1, Pallas kernels, attend(): pl.pallas_call(attend_kernel, out_shape=[jax.ShapeDtypeStruct((count, qua...  36 us
    pallas_call x1, Pallas kernels, outer_mean(): pl.pallas_call(partial(outer_kernel, group), out_shape=jax.ShapeDtypeStru...  23.9 us
    pallas_call x1, Pallas kernels, project(): pl.pallas_call(project_kernel, out_shape=[o[0] for o in outs], grid_spec=...  18.8 us
    all_to_all x1, blocking collectives, per_device(): lax.all_to_all(first.reshape(parts, count, block_rows * RANK), ('z', 'xl'...  14.6 us
    ppermute x1, waiting for transfers between devices, per_device(): first = lax.ppermute(first, ('y',) + HEAD_AXES, back)  14.6 us
    all_gather x1, blocking collectives, per_device(): first = lax.all_gather(first.reshape(parts * count, -1), 'y')  12.8 us
  transfers between devices with their start and end apart: 8, of which 6 were waited for; matrix products, arithmetic and copies ran while one was open for 4% of the time, Pallas kernels for 6%

profile of v1, /device:TPU:4, one launch (start us, length us, event | category | flops | bytes accessed | tf_op | source)
XLA Modules:
  0.0 365.7 jit_solution(3064062853930204054)
XLA Ops:
  7.2 1.0 copy.78
  8.2 0.9 reshape.79
  9.9 0.8 maximum_bitcast_fusion
  10.9 1.3 convert_reduce_fusion
  12.8 1.3 broadcast_multiply_fusion
  14.2 1.6 copy-done
  17.8 3.6 pair_bias.1
  21.5 5.0 %collective-permute-start = (f32[8,16,256]{2,1,0:T(8,128)S(1)}, f32[8,16,256]{2,1,0:T(8,128)S(1)}, u32[]{:S(2)}, u32[]{:S(2)}) collective-permute-start(f32[8,16,256]{2,1,0:T(8,128)S(1)} %pair_bias.1), channel_id=1, source_target_pairs={{0,0},{1,64},{2,128},{3,192},{4,4},{5,68},{6,132},{7,196},{64,1},{... | collective-permute-start | bytes 393224 | tf_op jit(solution)/shard_map/ppermute | solution.py:398
  26.5 2.0 collective-permute-start.1
  28.5 7.4 %collective-permute-done = f32[8,16,256]{2,1,0:T(8,128)S(1)} collective-permute-done((f32[8,16,256]{2,1,0:T(8,128)S(1)}, f32[8,16,256]{2,1,0:T(8,128)S(1)}, u32[]{:S(2)}, u32[]{:S(2)}) %collective-permute-start) | collective-permute-done | bytes 131104 | tf_op jit(solution)/shard_map/ppermute | solution.py:398
  35.9 7.6 %collective-permute-done.1 = f32[8,16,256]{2,1,0:T(8,128)S(1)} collective-permute-done((f32[8,16,256]{2,1,0:T(8,128)S(1)}, f32[8,16,256]{2,1,0:T(8,128)S(1)}, u32[]{:S(2)}, u32[]{:S(2)}) %collective-permute-start.1) | collective-permute-done | bytes 131104 | tf_op jit(solution)/shard_map/ppermute | solution.py:398
  43.5 0.7 pad_maximum_fusion.1
  44.5 1.3 slice.32
  46.4 0.8 fusion
  47.8 1.3 copy.72.wq
  49.2 1.3 copy.73.wg
  50.6 1.0 slice_reduce_fusion
  52.1 18.8 %project.1 = (bf16[4,8,128,1024]{3,2,1,0:T(8,128)(2,1)}, bf16[4,8,1024,128]{3,2,1,0:T(8,128)(2,1)}, bf16[4,8,256,128]{3,2,1,0:T(8,128)(2,1)}, f32[4,8,256,128]{3,2,1,0:T(8,128)}) custom-call(s32[2]{0:T(128)S(1)} %pad_add_fusion.place, f32[4,1024,256]{2,1,0:T(8,128)} %own.3, f32[4,1024,256]{2,1,0:T(8,128)} %own.3, f32[1,256]{1,0:T(1,128)S(1)} %bitcast.67, ...), custom_call_target="tpu_custom_call" | custom-call | tf_op jit(solution)/shard_map/project/pallas_call | solution.py:155
  70.9 1.1 select_maximum_fusion.merge
  72.0 70.9 %all-gather.12.cloned.1.call-done = f32[64,8,16,256]{3,2,1,0:T(8,128)} async-done(((f32[2,8,16,256]{3,2,1,0:T(8,128)}), f32[64,8,16,256]{3,2,1,0:T(8,128)}) %all-gather.12.cloned.1.call-update) | async-done | bytes 8388624 | tf_op jit(solution)/shard_map/all_gather | solution.py:399
  142.9 8.5 %copy.80 = f32[4,8,2,8,16,256]{5,4,3,2,0,1:T(8,128)} copy(f32[4,8,2,8,16,256]{5,4,3,2,1,0:T(8,128)} %bitcast.70) | data formatting | bytes 16777216 | tf_op jit(solution)/shard_map/reshape | solution.py:400
  151.4 36.0 %attend.1 = (f32[4,256,256]{2,1,0:T(8,128)}, f32[4,32,256]{2,1,0:T(8,128)S(1)}, f32[4,8192]{1,0:T(4,128)S(1)}) custom-call(s32[2]{0:T(128)S(1)} %pad_add_fusion.place, s32[256]{0:T(256)S(1)} %copy-done.7, f32[8,4,2,8,16,256]{5,4,3,2,1,0:T(8,128)} %bitcast.68, bf16[4,8,128,1024]{3,2,1,0:T(8,128)(2,1)} %get-tuple-element.9.kp, ...), custom_call_target="tpu_custom_call" | custom-call | tf_op jit(solution)/shard_map/attend/pallas_call | solution.py:227
  187.4 1.5 collective-permute-start.3
  188.9 3.8 %collective-permute-done.3 = f32[4,8192]{1,0:T(4,128)S(1)} collective-permute-done((f32[4,8192]{1,0:T(4,128)S(1)}, f32[4,8192]{1,0:T(4,128)S(1)}, u32[]{:S(2)}, u32[]{:S(2)}) %collective-permute-start.3) | collective-permute-done | bytes 131104 | tf_op jit(solution)/shard_map/ppermute | solution.py:409
  192.8 0.8 all_gather_reshape.7
  194.1 14.6 %all_to_all.5 = f32[16,4,512]{2,1,0:T(4,128)S(1)} all-to-all(f32[16,4,512]{2,1,0:T(4,128)S(1)} %copy.67), channel_id=1, replica_groups=mesh['y'=4,'z'=8,'xl'=2,'xh'=2,'c'=2] {'z','xl'}, dimensions={0} | all-to-all | bytes 262144 | tf_op jit(solution)/shard_map/all_to_all | solution.py:414
  208.8 12.8 %all_gather.26 = f32[4,64,512]{2,1,0:T(8,128)S(1)} all-gather(f32[1,64,512]{2,1,0:T(8,128)S(1)} %all_gather_reshape.6), channel_id=1, replica_groups=mesh['y'=4,'z'=8,'xl'=2,'xh'=2,'c'=2] {'y'}, dimensions={0}, use_global_device_ids=true | all-gather | bytes 655360 | tf_op jit(solution)/shard_map/all_gather | solution.py:415
  221.6 3.6 collective-permute-start.2
  225.9 14.6 %collective-permute-done.2 = f32[4,64,512]{2,1,0:T(8,128)S(1)} collective-permute-done((f32[4,64,512]{2,1,0:T(8,128)S(1)}, f32[4,64,512]{2,1,0:T(8,128)S(1)}, u32[]{:S(2)}, u32[]{:S(2)}) %collective-permute-start.2) | collective-permute-done | bytes 524320 | tf_op jit(solution)/shard_map/ppermute | solution.py:417
  240.5 92.7 %all-gather.10.cloned.1.call-done = f32[32,8,8192]{2,1,0:T(8,128)} async-done(((f32[1,8,8192]{2,1,0:T(8,128)}), f32[32,8,8192]{2,1,0:T(8,128)}) %all-gather.10.cloned.1.call-update) | async-done | bytes 8388624 | tf_op jit(solution)/shard_map/all_gather | solution.py:410
  333.2 23.9 %outer_mean.1 = f32[16,256,128]{2,1,0:T(8,128)} custom-call(s32[2]{0:T(128)S(1)} %pad_add_fusion.place, s32[1024]{0:T(1024)S(1)} %copy-done.2, f32[256,512]{1,0:T(8,128)S(1)} %bitcast.58, f32[256,8192]{1,0:T(8,128)} %bitcast.69, f32[128,1024]{1,0:T(8,128)S(1)} %copy.69.weight_t, f32[128,1]{1,0:T(8,128)S(1)} %copy.70.out_bias, f32[4,1,256]{2,1,0:T(1,128)S(1)} %bitcast.62, ...), custom_call_target="tpu_custom_call" | custom-call | tf_op jit(solution)/shard_map/outer_mean/pallas_call | solution.py:300
  357.1 2.0 copy.82
  (61 shorter events, 7.1 us)
Async XLA Ops:
  7.2 37.3 %copy-start.2 = (s32[1024]{0:T(1024)S(1)}, s32[1024]{0:T(1024)}, u32[]{:S(2)}) copy-start(s32[1024]{0:T(1024)} %mask_s.1) | copy-start | bytes 12292
  7.2 37.4 %all-gather.14.cloned.1.call-start = ((), (), s32[]{:S(2)}) async-start(), calls=%async_computation.4 | async-start | bytes 1802240 | tf_op jit(solution)/shard_map/all_gather | solution.py:369
  10.7 132.2 %all-gather.12.cloned.1.call-start = ((), (), s32[]{:S(2)}) async-start(), calls=%async_computation.3 | async-start | bytes 8650752 | tf_op jit(solution)/shard_map/all_gather | solution.py:399
  14.2 1.6 copy-start
  15.8 0.7 copy-start.3
  16.5 0.7 copy-start.4
  17.1 0.7 copy-start.5
  21.5 14.4 %collective-permute-start = (f32[8,16,256]{2,1,0:T(8,128)S(1)}, f32[8,16,256]{2,1,0:T(8,128)S(1)}, u32[]{:S(2)}, u32[]{:S(2)}) collective-permute-start(f32[8,16,256]{2,1,0:T(8,128)S(1)} %pair_bias.1), channel_id=1, source_target_pairs={{0,0},{1,64},{2,128},{3,192},{4,4},{5,68},{6,132},{7,196},{64,1},{... | collective-permute-start | bytes 393224 | tf_op jit(solution)/shard_map/ppermute | solution.py:398
  26.5 17.0 %collective-permute-start.1 = (f32[8,16,256]{2,1,0:T(8,128)S(1)}, f32[8,16,256]{2,1,0:T(8,128)S(1)}, u32[]{:S(2)}, u32[]{:S(2)}) collective-permute-start(f32[8,16,256]{2,1,0:T(8,128)S(1)} %pair_bias.1), channel_id=1, source_target_pairs={{0,4},{1,68},{2,132},{3,196},{4,0},{5,64},{6,128},{7,192},{64,5},{... | collective-permute-start | bytes 393224 | tf_op jit(solution)/shard_map/ppermute | solution.py:398
  44.3 181.6 %all-gather.8.cloned.1.call-start = ((), (), s32[]{:S(2)}) async-start(), calls=%async_computation.1 | async-start | bytes 5242880 | tf_op jit(solution)/shard_map/all_gather | solution.py:420
  47.6 4.0 %slice-start = ((f32[4,1288,64]{1,2,0:T(8,128)}), f32[4,256,64]{1,2,0:T(8,128)S(1)}, s32[]{:S(2)}) async-start(f32[4,1288,64]{1,2,0:T(8,128)} %all-gather.14.cloned.1.call-done), calls=%async_computation.5 | async-start | bytes 524288 | tf_op jit(solution)/shard_map/slice | solution.py:372
  47.8 4.4 %copy-start.6 = (f32[256]{0:T(256)S(1)}, f32[256]{0:T(256)}, u32[]{:S(2)}) copy-start(f32[256]{0:T(256)} %param.17) | copy-start | bytes 3076
  142.9 8.5 %copy-start.1 = (f32[2,256,32]{1,2,0:T(8,128)S(1)}, f32[2,256,32]{1,2,0:T(8,128)}, u32[]{:S(2)}) copy-start(f32[2,256,32]{1,2,0:T(8,128)} %param.23) | copy-start | bytes 196612
  142.9 8.5 %copy-start.7 = (s32[256]{0:T(256)S(1)}, s32[256]{0:T(256)}, u32[]{:S(2)}) copy-start(s32[256]{0:T(256)} %flags_s.1) | copy-start | bytes 3076
  187.3 37.9 %copy-start.9 = (f32[1024,128]{1,0:T(8,128)S(1)}, f32[1024,128]{1,0:T(8,128)}, u32[]{:S(2)}) copy-start(f32[1024,128]{1,0:T(8,128)} %param.24) | copy-start | bytes 1572868
  187.3 38.4 %copy-start.10 = (f32[128]{0:T(128)S(1)}, f32[128]{0:T(128)}, u32[]{:S(2)}) copy-start(f32[128]{0:T(128)} %param.25) | copy-start | bytes 1540
  187.3 145.9 %all-gather.10.cloned.1.call-start = ((), (), s32[]{:S(2)}) async-start(), calls=%async_computation.2 | async-start | bytes 8650752 | tf_op jit(solution)/shard_map/all_gather | solution.py:410
  187.4 5.3 %collective-permute-start.3 = (f32[4,8192]{1,0:T(4,128)S(1)}, f32[4,8192]{1,0:T(4,128)S(1)}, u32[]{:S(2)}, u32[]{:S(2)}) collective-permute-start(f32[4,8192]{1,0:T(4,128)S(1)} %get-tuple-element.15), channel_id=1, source_target_pairs={{0,4},{4,0},{1,5},{5,1},{2,6},{6,2},{3,7},{7,3},{8,12},{12,8},{9,1... | collective-permute-start | bytes 393224 | tf_op jit(solution)/shard_map/ppermute | solution.py:409
  221.6 18.9 %collective-permute-start.2 = (f32[4,64,512]{2,1,0:T(8,128)S(1)}, f32[4,64,512]{2,1,0:T(8,128)S(1)}, u32[]{:S(2)}, u32[]{:S(2)}) collective-permute-start(f32[4,64,512]{2,1,0:T(8,128)S(1)} %all_gather.26), channel_id=1, source_target_pairs={{0,0},{1,64},{2,128},{3,192},{64,1},{65,65},{66,129},{67,193},{128... | collective-permute-start | bytes 1572872 | tf_op jit(solution)/shard_map/ppermute | solution.py:417
  333.2 23.9 %copy-start.8 = (f32[4,1024,256]{2,1,0:T(8,128)S(1)}, f32[4,1024,256]{2,1,0:T(8,128)}, u32[]{:S(2)}) copy-start(f32[4,1024,256]{2,1,0:T(8,128)} %all-gather.8.cloned.1.call-done) | copy-start | bytes 12582916
Sparse Core Ops, SparseCore 0:
  10.8 27.1 all-gather.13
  44.4 98.4 all-gather.11
  187.5 36.8 all-gather.7
  227.3 105.8 all-gather.9
